TPU v7x, 32 devices: a whole 2x2x4 slice. The times are simulated.
32 devices in a mesh: gx: 8 (over z, core), gy: 4 (over y, x).
Axes of the slice: x: 2, y: 2, z: 4, core: 2. Of those that a mesh axis runs over, the one named last changes fastest.
Arguments:
- adjoint_field: float32 [3, 8, 4, 64, 512], P(None, 'gx', 'gy'), may hold values from -12 to 27
- velocity: bfloat16 [3, 8, 4, 64, 512], P(None, 'gx', 'gy'), may hold values from -1.1953125 to 1.1953125
- diffusivity: float32 [3, 8, 4, 64, 512], P(None, 'gx', 'gy'), may hold values from 0.3 to 3
- jacobian: float32 [8, 4, 64, 512], P('gx', 'gy'), may hold values from 0.5 to 2
- element_slot: int32 [8, 4, 64], P('gx', 'gy'), may hold values from 0 to 63, each once within a row
Outputs:
- adjoint_prev: float32 [3, 8, 4, 64, 512], P(None, 'gx', 'gy')
Inputs may be any that keep to these rules, and one draw needn't show every extreme that they name: Each partition's row of element_slot is a permutation of 0 to 63.
All inputs are finite; a program needn't handle non-finite values.
Results may differ from a plain program's by a relative error of at most 0.0003.
Values sent between devices are 32-bit elements; how exact they have to be, the bound alone decides.
A program may use at most 64 MiB of HBM per device.

v0:
```python
import functools

import jax
import jax.numpy as jnp
import numpy as np
from jax import lax
from jax.experimental import pallas as pl
from jax.experimental.pallas import tpu as pltpu
from jax.sharding import PartitionSpec as P

EX = 2
EY = 2
EZ = 16
ITERS = 4

time_step = 0.25
MESH = pl.DeviceIdType.MESH
f32 = jnp.float32
bf16 = jnp.bfloat16

SIDES = ((-1, 0), (1, 0), (0, -1), (0, 1))
CORNERS = ((-1, -1), (-1, 1), (1, -1), (1, 1))


def legendre_seven(points):
    previous = points * 0.0 + 1.0
    current = points
    for degree in range(1, 7):
        following = ((2 * degree + 1) * points * current - degree * previous) / (degree + 1)
        previous = current
        current = following
    return current


def gll_tables():
    poly_order = 7
    points = np.array(
        [
            -1.0,
            -0.8717401485096066,
            -0.5917001814331423,
            -0.2092992179024789,
            0.2092992179024789,
            0.5917001814331423,
            0.8717401485096066,
            1.0,
        ]
    )
    end_values = legendre_seven(points)
    weights = 2.0 / (poly_order * (poly_order + 1) * end_values**2)
    spread = points[:, None] - points[None, :]
    identity = np.eye(poly_order + 1)
    diff_table = end_values[:, None] / (end_values[None, :] * (spread + identity))
    diff_table = diff_table * (1.0 - identity)
    corners = np.zeros(poly_order + 1)
    corners[0] = -poly_order * (poly_order + 1) / 4.0
    corners[-1] = poly_order * (poly_order + 1) / 4.0
    diff_table = diff_table + identity * corners[None, :]
    return (weights.astype(np.float32), diff_table.astype(np.float32))


def halves(table):
    high = table.astype(jnp.bfloat16)
    low = (table - high.astype(np.float32)).astype(jnp.bfloat16)
    return high, low


def constant_tables():
    weights, diff = gll_tables()
    eye = np.eye(8, dtype=np.float32)
    pair = np.eye(2, dtype=np.float32)
    along_j = np.kron(pair, np.kron(diff.T, eye))
    along_k = np.kron(pair, np.kron(eye, diff.T))
    forward = np.concatenate([along_j, along_k], axis=1)
    f_high, f_low = halves(forward)
    b_high, b_low = halves(np.ascontiguousarray(forward.T))
    forward_high = np.concatenate([f_high, f_high], axis=0)
    backward_both = np.concatenate([b_high, b_low], axis=1)
    coef = np.zeros((2, 2, 4, 4, 128), np.float32)
    for flip in range(2):
        matrix = diff.T if flip else diff
        for out in range(4):
            for inn in range(4):
                for il in range(2):
                    span = slice(il * 64, il * 64 + 64)
                    coef[flip, 0, out, inn, span] = matrix[2 * out + il, 2 * inn + il]
                    coef[flip, 1, out, inn, span] = matrix[2 * out + il, 2 * inn + 1 - il]
    coef = coef.reshape(64, 128)
    cube = weights[:, None, None] * weights[None, :, None] * weights[None, None, :]
    return forward_high, f_low, backward_both, b_high, coef, cube.reshape(4, 128).astype(np.float32)


def dot(a, b):
    return jnp.dot(a, b, preferred_element_type=f32)


def split(values):
    high = values.astype(bf16)
    return high, (values - high.astype(f32)).astype(bf16)


def roll(values, shift, axis=None):
    axis = values.ndim - 1 if axis is None else axis
    shift = shift % values.shape[axis]
    return values if shift == 0 else pltpu.roll(values, shift, axis)


def kernel(
    nx,
    ny,
    adj_ref,
    vel_ref,
    dif_ref,
    jac_ref,
    slot_ref,
    fh_ref,
    fl_ref,
    bb_ref,
    bh_ref,
    coef_ref,
    cube_ref,
    out_ref,
    mass,
    cond,
    share,
    w,
    res,
    dire,
    along,
    sol,
    face_out,
    face_in,
    corner_out,
    corner_in,
    sums,
    face_s,
    face_r,
    corner_s,
    corner_r,
    sums_s,
    sums_r,
):
    gx = lax.axis_index("gx")
    gy = lax.axis_index("gy")
    total = nx * ny
    me = gx * ny + gy
    cells = EX * EY * EZ

    face_in[...] = jnp.zeros_like(face_in)
    corner_in[...] = jnp.zeros_like(corner_in)

    barrier = pltpu.get_barrier_semaphore()

    def greet(step, carry):
        other = lax.rem(me + step, total)
        pl.semaphore_signal(
            barrier, inc=1, device_id=(other // ny, lax.rem(other, ny)), device_id_type=MESH
        )
        return carry

    lax.fori_loop(1, total, greet, 0)

    lane = lax.broadcasted_iota(jnp.int32, (1, 128), 1)
    lane_k = lane % 8
    lane_j = (lane // 8) % 8
    lane_i = lane // 64
    group = lane // 8

    place = lax.broadcasted_iota(jnp.int32, (cells, cells), 0)
    picks = (jnp.broadcast_to(slot_ref[...], (cells, cells)) == place).astype(f32)
    pick = picks.astype(bf16)

    def to_brick(stored):
        high, rest = split(stored)
        low = rest
        third = (stored - high.astype(f32) - low.astype(f32)).astype(bf16)
        return dot(pick, high) + dot(pick, low) + dot(pick, third)

    def rows(values):
        return values.reshape(values.shape[0] * values.shape[1], 128)

    def derive_jk(values):
        high, low = split(values)
        both = dot(jnp.concatenate([high, low], axis=1), fh_ref[...]) + dot(high, fl_ref[...])
        return both[:, :128], both[:, 128:]

    def derive_i(parts, flip):
        turned = [roll(part, 64) for part in parts]
        outs = []
        for out in range(4):
            acc = None
            for inn in range(4):
                at = flip * 32 + out * 4 + inn
                term = parts[inn] * coef_ref[at : at + 1, :]
                term = term + turned[inn] * coef_ref[at + 16 : at + 17, :]
                acc = term if acc is None else acc + term
            outs.append(acc)
        return outs

    adj = [to_brick(adj_ref[c]) for c in range(3)]
    for h in range(4):
        for c in range(3):
            w[h, c] = adj[c][:, h * 128 : h * 128 + 128].reshape(EX, EY, EZ, 128)
    jac = to_brick(jac_ref[0])
    for h in range(4):
        weight = cube_ref[h : h + 1, :]
        mass[h] = jac[:, h * 128 : h * 128 + 128] * weight
    for m in range(3):
        con = to_brick(dif_ref[m])
        for h in range(4):
            weight = time_step * cube_ref[h : h + 1, :]
            cond[m, h] = con[:, h * 128 : h * 128 + 128] * weight

    first_x = jnp.where(gx > 0, 0.5, 1.0).astype(f32)
    last_x = jnp.where(gx < nx - 1, 0.5, 1.0).astype(f32)
    first_y = jnp.where(gy > 0, 0.5, 1.0).astype(f32)
    last_y = jnp.where(gy < ny - 1, 0.5, 1.0).astype(f32)
    row_z = lax.broadcasted_iota(jnp.int32, (EZ, 128), 0)
    lane_z = lax.broadcasted_iota(jnp.int32, (EZ, 128), 1)
    k_z = lane_z % 8
    half_z = ((k_z == 0) & (row_z > 0)) | ((k_z == 7) & (row_z < EZ - 1))
    share_z = jnp.where(half_z, 0.5, 1.0).astype(f32)
    for x in range(EX):
        low_x = first_x if x == 0 else 0.5
        top_x = last_x if x == EX - 1 else 0.5
        for y in range(EY):
            low_y = first_y if y == 0 else 0.5
            top_y = last_y if y == EY - 1 else 0.5
            share_y = jnp.where(lane_j == 0, low_y, jnp.where(lane_j == 7, top_y, 1.0))
            for h in range(4):
                share_x = jnp.ones((1, 128), f32)
                if h == 0:
                    share_x = jnp.where(lane_i == 0, low_x, 1.0)
                if h == 3:
                    share_x = jnp.where(lane_i == 1, top_x, 1.0)
                at = (x * EY + y) * EZ
                share[h, at : at + EZ] = share_z * (share_x * share_y)

    dire[...] = jnp.zeros_like(dire)
    along[...] = jnp.zeros_like(along)
    sol[...] = jnp.zeros_like(sol)

    full = w[...].reshape(4, 3, cells, 128)
    grad_j, grad_k = derive_jk(full.reshape(12 * cells, 128))
    grad_j = grad_j.reshape(4, 3, cells, 128)
    grad_k = grad_k.reshape(4, 3, cells, 128)
    grad_i = [derive_i([full[h, c] for h in range(4)], 0) for c in range(3)]
    flow = [dot(pick, vel_ref[c]) for c in range(3)]
    for h in range(4):
        at = slice(h * 128, h * 128 + 128)
        v = [flow[c][:, at] for c in range(3)]
        r = [
            grad_j[h, 2] - grad_k[h, 1],
            grad_k[h, 0] - grad_i[2][h],
            grad_i[1][h] - grad_j[h, 0],
        ]
        for c in range(3):
            c1, c2 = (c + 1) % 3, (c + 2) % 3
            value = full[h, c] + time_step * (v[c1] * r[c2] - v[c2] * r[c1])
            w[h, c] = (mass[h] * value).reshape(EX, EY, EZ, 128)

    pl.semaphore_wait(barrier, total - 1)

    def exists(side):
        ax, ay = gx + side[0], gy + side[1]
        return (ax >= 0) & (ax < nx) & (ay >= 0) & (ay < ny)

    def copies(turn):
        made = []
        for d, side in enumerate(SIDES):
            made.append(
                (
                    side,
                    pltpu.make_async_remote_copy(
                        src_ref=face_out.at[turn, d],
                        dst_ref=face_in.at[turn, d],
                        send_sem=face_s.at[turn, d],
                        recv_sem=face_r.at[turn, d],
                        device_id=(gx + side[0], gy + side[1]),
                        device_id_type=MESH,
                    ),
                )
            )
        for d, side in enumerate(CORNERS):
            made.append(
                (
                    side,
                    pltpu.make_async_remote_copy(
                        src_ref=corner_out.at[turn, d],
                        dst_ref=corner_in.at[turn, d],
                        send_sem=corner_s.at[turn, d],
                        recv_sem=corner_r.at[turn, d],
                        device_id=(gx + side[0], gy + side[1]),
                        device_id_type=MESH,
                    ),
                )
            )
        return made

    def corner_spot(side):
        h = 0 if side[0] < 0 else 3
        x = 0 if side[0] < 0 else EX - 1
        y = 0 if side[1] < 0 else EY - 1
        base = (0 if side[0] < 0 else 64) + (0 if side[1] < 0 else 56)
        return h, x, y, base

    def fold_inside():
        values = w[...].reshape(12 * cells, 128)
        count = 12 * cells
        zed = lax.broadcasted_iota(jnp.int32, (EZ, 128), 0)
        kay = lax.broadcasted_iota(jnp.int32, (EZ, 128), 1) % 8
        upper = ((kay == 7) & (zed < EZ - 1)).astype(f32)
        lower = ((kay == 0) & (zed > 0)).astype(f32)
        from_next = roll(roll(values, 7), count - 1, 0).reshape(12 * EX * EY, EZ, 128)
        from_last = roll(roll(values, -7), 1, 0).reshape(12 * EX * EY, EZ, 128)
        values = values.reshape(12 * EX * EY, EZ, 128)
        values = values + from_next * upper[None] + from_last * lower[None]
        values = values.reshape(4, 3, EX, EY, EZ, 128)
        is_top = lane_j == 7
        is_low = lane_j == 0
        columns = [values[:, :, :, y] for y in range(EY)]
        folded = list(columns)
        for y in range(EY - 1):
            folded[y] = folded[y] + jnp.where(is_top, roll(columns[y + 1], 56), 0.0)
            folded[y + 1] = folded[y + 1] + jnp.where(is_low, roll(columns[y], -56), 0.0)
        for y in range(EY):
            w[:, :, :, y] = folded[y]
        for x in range(EX - 1):
            left = w[3, :, x]
            right = w[0, :, x + 1]
            w[3, :, x] = left + jnp.where(lane_i == 1, roll(right, 64), 0.0)
            w[0, :, x + 1] = right + jnp.where(lane_i == 0, roll(left, 64), 0.0)

    def send_faces(turn):
        left = w[0, :, 0]
        face_out[turn, 0] = jnp.where(lane_i == 0, left[:, 0], roll(left[:, 1], 64))
        right = w[3, :, EX - 1]
        face_out[turn, 1] = jnp.where(lane_i == 0, roll(right[:, 0], 64), right[:, 1])
        for d, y, j in ((2, 0, 0), (3, EY - 1, 7)):
            acc = None
            for h in range(4):
                for x in range(EX):
                    part = jnp.where(lane_j == j, w[h, :, x, y], 0.0)
                    part = roll(part, h * 8 + x * 32 - j * 8)
                    acc = part if acc is None else acc + part
            face_out[turn, d] = acc
        for d, side in enumerate(CORNERS):
            h, x, y, base = corner_spot(side)
            acc = None
            for c in range(3):
                part = jnp.where(group == base // 8, w[h, c, x, y], 0.0)
                part = roll(part, c * 8 - base)
                acc = part if acc is None else acc + part
            corner_out[turn, d] = acc
        for side, copy in copies(turn):
            pl.when(exists(side))(copy.start)

    def take_faces(turn):
        for side, copy in copies(turn):
            pl.when(exists((-side[0], -side[1])))(copy.wait_recv)
        left = face_in[turn, 1]
        right = face_in[turn, 0]
        for h, x, arrived, here in ((0, 0, left, 0), (3, EX - 1, right, 1)):
            turned = roll(arrived, 64)
            pair = (arrived, turned) if here == 0 else (turned, arrived)
            for y in range(EY):
                w[h, :, x, y] = w[h, :, x, y] + jnp.where(lane_i == here, pair[y], 0.0)
        for d, y, j in ((3, 0, 0), (2, EY - 1, 7)):
            arrived = face_in[turn, d]
            for h in range(4):
                for x in range(EX):
                    part = roll(arrived, j * 8 - h * 8 - x * 32)
                    w[h, :, x, y] = w[h, :, x, y] + jnp.where(lane_j == j, part, 0.0)
        for d, side in enumerate(CORNERS):
            h, x, y, base = corner_spot((-side[0], -side[1]))
            arrived = corner_in[turn, d]
            for c in range(3):
                part = roll(arrived, base - c * 8)
                w[h, c, x, y] = w[h, c, x, y] + jnp.where(group == base // 8, part, 0.0)

    def sent_faces(turn):
        for side, copy in copies(turn):
            pl.when(exists(side))(copy.wait_send)

    fold_inside()
    send_faces(0)
    take_faces(0)
    sent_faces(0)
    res[...] = w[...]

    def sum_copy(turn, step):
        other = lax.rem(me + step, total)
        return pltpu.make_async_remote_copy(
            src_ref=sums.at[turn, me],
            dst_ref=sums.at[turn, me],
            send_sem=sums_s.at[turn],
            recv_sem=sums_r.at[turn],
            device_id=(other // ny, lax.rem(other, ny)),
            device_id_type=MESH,
        )

    def iteration(turn, carry):
        norm_last, step_last = carry
        values = res[...].reshape(4, 3, cells, 128)
        grad_j, grad_k = derive_jk(values.reshape(12 * cells, 128))
        flux_j = (grad_j.reshape(4, 3, cells, 128) * cond[1][:, None]).reshape(12 * cells, 128)
        flux_k = (grad_k.reshape(4, 3, cells, 128) * cond[2][:, None]).reshape(12 * cells, 128)
        high, low = split(jnp.concatenate([flux_j, flux_k], axis=1))
        both = dot(high, bb_ref[...])
        stiff = both[:, :128] + both[:, 128:] + dot(low, bh_ref[...])
        stiff = stiff.reshape(4, 3, cells, 128)
        norm = jnp.zeros((cells, 128), f32)
        product = jnp.zeros((cells, 128), f32)
        for c in range(3):
            grads = derive_i([values[h, c] for h in range(4)], 0)
            fluxes = [grads[h] * cond[0, h] for h in range(4)]
            backs = derive_i(fluxes, 1)
            for h in range(4):
                here = values[h, c]
                applied = mass[h] * here + stiff[h, c] + backs[h]
                norm = norm + here * here * share[h]
                product = product + here * applied
                w[h, c] = applied.reshape(EX, EY, EZ, 128)
        norm = jnp.sum(norm, axis=0, keepdims=True)
        product = jnp.sum(product, axis=0, keepdims=True)
        sums[turn, me] = jnp.concatenate([norm, product], axis=0)

        def send(step, inner):
            sum_copy(turn, step).start()
            return inner

        lax.fori_loop(1, total, send, 0)

        @pl.when(turn < ITERS - 1)
        def _():
            fold_inside()
            send_faces(turn + 1)
            take_faces(turn + 1)
            sent_faces(turn + 1)

        arrived = sums.at[turn, pl.ds(0, total - 1)]
        pltpu.make_async_copy(arrived, arrived, sums_r.at[turn]).wait()
        gathered = jnp.sum(sums[turn], axis=0)
        totals = jnp.sum(gathered, axis=1, keepdims=True)
        norm = totals[0:1]
        product = totals[1:2]
        ratio = jnp.where(turn == 0, 0.0, norm / norm_last)
        step_len = norm / (product - ratio * norm / step_last)
        for h in range(4):
            moved = res[h] + ratio * dire[h]
            dire[h] = moved
            sol[h] = sol[h] + step_len * moved

            @pl.when(turn < ITERS - 1)
            def _():
                trail = w[h] + ratio * along[h]
                along[h] = trail
                res[h] = res[h] - step_len * trail

        pltpu.make_async_copy(arrived, arrived, sums_s.at[turn]).wait()
        return norm, step_len

    one = jnp.ones((1, 1), f32)
    lax.fori_loop(0, ITERS, iteration, (one, one))

    back = picks.T.astype(bf16)
    for c in range(3):
        parts = [sol[h, c].reshape(cells, 128) for h in range(4)]
        whole = jnp.concatenate(parts, axis=1)
        high, low = split(whole)
        third = (whole - high.astype(f32) - low.astype(f32)).astype(bf16)
        out_ref[c] = dot(back, high) + dot(back, low) + dot(back, third)


def local(nx, ny, adjoint_field, velocity, diffusivity, jacobian, element_slot):
    tables = [jnp.asarray(table) for table in constant_tables()]
    cells = element_slot.size
    nodes = adjoint_field.shape[-1]
    field = (4, 3, EX, EY, EZ, 128)
    vmem = pl.BlockSpec(memory_space=pltpu.VMEM)
    result = pl.pallas_call(
        functools.partial(kernel, nx, ny),
        out_shape=jax.ShapeDtypeStruct((3, cells, nodes), f32),
        in_specs=[vmem] * 11,
        out_specs=vmem,
        scratch_shapes=[
            pltpu.VMEM((4, cells, 128), f32),
            pltpu.VMEM((3, 4, cells, 128), f32),
            pltpu.VMEM((4, cells, 128), f32),
            pltpu.VMEM(field, f32),
            pltpu.VMEM(field, f32),
            pltpu.VMEM(field, f32),
            pltpu.VMEM(field, f32),
            pltpu.VMEM(field, f32),
            pltpu.VMEM((ITERS, 4, 3, EZ, 128), f32),
            pltpu.VMEM((ITERS, 4, 3, EZ, 128), f32),
            pltpu.VMEM((ITERS, 4, EZ, 128), f32),
            pltpu.VMEM((ITERS, 4, EZ, 128), f32),
            pltpu.VMEM((ITERS, nx * ny, 2, 128), f32),
            pltpu.SemaphoreType.DMA((ITERS, 4)),
            pltpu.SemaphoreType.DMA((ITERS, 4)),
            pltpu.SemaphoreType.DMA((ITERS, 4)),
            pltpu.SemaphoreType.DMA((ITERS, 4)),
            pltpu.SemaphoreType.DMA((ITERS,)),
            pltpu.SemaphoreType.DMA((ITERS,)),
        ],
        compiler_params=pltpu.CompilerParams(
            collective_id=0, has_side_effects=True, vmem_limit_bytes=48 * 1024 * 1024
        ),
    )(
        adjoint_field.reshape(3, cells, nodes),
        velocity.reshape(3, cells, nodes),
        diffusivity.reshape(3, cells, nodes),
        jacobian.reshape(1, cells, nodes),
        element_slot.reshape(1, cells),
        *tables,
    )
    return result.reshape(3, 1, 1, cells, nodes)


def solution(mesh):
    in_specs = (
        P(None, "gx", "gy", None, None),
        P(None, "gx", "gy", None, None),
        P(None, "gx", "gy", None, None),
        P("gx", "gy", None, None),
        P("gx", "gy", None),
    )
    out_specs = P(None, "gx", "gy", None, None)
    run = functools.partial(local, mesh.shape["gx"], mesh.shape["gy"])
    return jax.shard_map(run, mesh=mesh, in_specs=in_specs, out_specs=out_specs, check_vma=False)
```

profile of v0, /device:TPU:0, one launch (start us, length us, event | category | flops | bytes accessed | tf_op | source)
XLA Modules:
  0.0 47.7 jit_solution(2396046008700737610)
XLA Ops:
  0.0 0.0 copy-start.9
  0.0 0.0 copy-start.10
  0.0 0.7 %copy-done.9 = f32[4,128]{1,0:T(4,128)S(1)} copy-done((f32[4,128]{1,0:T(4,128)S(1)}, f32[4,128]{1,0:T(4,128)}, u32[]{:S(2)}) %copy-start.9) | copy-done | bytes 2072
  0.7 0.0 copy-done.10
  0.7 0.0 copy-start
  0.7 1.0 %copy-done = f32[3,1,1,64,512]{4,3,2,1,0:T(8,128)S(1)} copy-done((f32[3,1,1,64,512]{4,3,2,1,0:T(8,128)S(1)}, f32[3,1,1,64,512]{4,3,2,1,0:T(8,128)}, u32[]{:S(2)}) %copy-start) | copy-done | bytes 393240
  1.7 0.0 copy-start.1
  1.7 1.0 %copy-done.1 = f32[3,1,1,64,512]{4,3,2,1,0:T(8,128)S(1)} copy-done((f32[3,1,1,64,512]{4,3,2,1,0:T(8,128)S(1)}, f32[3,1,1,64,512]{4,3,2,1,0:T(8,128)}, u32[]{:S(2)}) %copy-start.1) | copy-done | bytes 393240
  2.7 0.0 copy-start.2
  2.7 0.9 %copy-done.2 = bf16[3,1,1,64,512]{4,3,2,1,0:T(8,128)(2,1)S(1)} copy-done((bf16[3,1,1,64,512]{4,3,2,1,0:T(8,128)(2,1)S(1)}, bf16[3,1,1,64,512]{4,3,2,1,0:T(8,128)(2,1)}, u32[]{:S(2)}) %copy-start.2) | copy-done | bytes 196632
  3.6 0.0 copy-start.3
  3.6 0.9 %copy-done.3 = f32[1,1,64,512]{3,2,1,0:T(8,128)S(1)} copy-done((f32[1,1,64,512]{3,2,1,0:T(8,128)S(1)}, f32[1,1,64,512]{3,2,1,0:T(8,128)}, u32[]{:S(2)}) %copy-start.3) | copy-done | bytes 131096
  4.5 0.0 copy-start.4
  4.5 0.9 %copy-done.4 = bf16[256,256]{1,0:T(8,128)(2,1)S(1)} copy-done((bf16[256,256]{1,0:T(8,128)(2,1)S(1)}, bf16[256,256]{1,0:T(8,128)(2,1)}, u32[]{:S(2)}) %copy-start.4) | copy-done | bytes 131096
  5.4 0.0 copy-start.5
  5.4 0.9 %copy-done.5 = bf16[256,256]{1,0:T(8,128)(2,1)S(1)} copy-done((bf16[256,256]{1,0:T(8,128)(2,1)S(1)}, bf16[256,256]{1,0:T(8,128)(2,1)}, u32[]{:S(2)}) %copy-start.5) | copy-done | bytes 131096
  6.3 0.0 copy-start.6
  6.3 0.8 %copy-done.6 = bf16[256,128]{1,0:T(8,128)(2,1)S(1)} copy-done((bf16[256,128]{1,0:T(8,128)(2,1)S(1)}, bf16[256,128]{1,0:T(8,128)(2,1)}, u32[]{:S(2)}) %copy-start.6) | copy-done | bytes 65560
  7.2 0.0 copy-start.7
  7.2 0.8 %copy-done.7 = bf16[128,256]{1,0:T(8,128)(2,1)S(1)} copy-done((bf16[128,256]{1,0:T(8,128)(2,1)S(1)}, bf16[128,256]{1,0:T(8,128)(2,1)}, u32[]{:S(2)}) %copy-start.7) | copy-done | bytes 65560
  8.0 0.0 copy-start.8
  8.0 0.8 %copy-done.8 = f32[64,128]{1,0:T(8,128)S(1)} copy-done((f32[64,128]{1,0:T(8,128)S(1)}, f32[64,128]{1,0:T(8,128)}, u32[]{:S(2)}) %copy-start.8) | copy-done | bytes 32792
  8.8 38.1 %shard_map.109 = f32[3,64,512]{2,1,0:T(8,128)S(1)} custom-call(f32[3,64,512]{2,1,0:T(8,128)S(1)} %bitcast.9, bf16[3,64,512]{2,1,0:T(8,128)(2,1)S(1)} %bitcast.11, f32[3,64,512]{2,1,0:T(8,128)S(1)} %bitcast.10, f32[1,64,512]{2,1,0:T(8,128)S(1)} %bitcast.12, s32[1,64]{1,0:T(1,128)S(1)} %bitcast.13, bf16[256,256]{1,0:T(8,128)(2,1)S(1)} %copy-done.5, ...), custom_call_target="tpu_custom_call" | custom-call | tf_op jit(solution)/shard_map/pallas_call | solution.py:481
  46.9 0.7 %copy.14 = f32[3,1,1,64,512]{4,3,2,1,0:T(8,128)} copy(f32[3,1,1,64,512]{4,3,2,1,0:T(8,128)S(1)} %bitcast.8) | data formatting | bytes 786432
Async XLA Ops:
  0.0 0.7 %copy-start.9 = (f32[4,128]{1,0:T(4,128)S(1)}, f32[4,128]{1,0:T(4,128)}, u32[]{:S(2)}) copy-start(f32[4,128]{1,0:T(4,128)} %constant.17.clone.cube_ref) | copy-start | bytes 6148
  0.0 0.7 %copy-start.10 = (s32[1,1,64]{2,1,0:T(1,128)S(1)}, s32[1,1,64]{2,1,0:T(1,128)}, u32[]{:S(2)}) copy-start(s32[1,1,64]{2,1,0:T(1,128)} %param.15) | copy-start | bytes 772
  0.7 1.0 %copy-start = (f32[3,1,1,64,512]{4,3,2,1,0:T(8,128)S(1)}, f32[3,1,1,64,512]{4,3,2,1,0:T(8,128)}, u32[]{:S(2)}) copy-start(f32[3,1,1,64,512]{4,3,2,1,0:T(8,128)} %param.11) | copy-start | bytes 1179652
  1.7 1.0 %copy-start.1 = (f32[3,1,1,64,512]{4,3,2,1,0:T(8,128)S(1)}, f32[3,1,1,64,512]{4,3,2,1,0:T(8,128)}, u32[]{:S(2)}) copy-start(f32[3,1,1,64,512]{4,3,2,1,0:T(8,128)} %param.13) | copy-start | bytes 1179652
  2.7 0.9 %copy-start.2 = (bf16[3,1,1,64,512]{4,3,2,1,0:T(8,128)(2,1)S(1)}, bf16[3,1,1,64,512]{4,3,2,1,0:T(8,128)(2,1)}, u32[]{:S(2)}) copy-start(bf16[3,1,1,64,512]{4,3,2,1,0:T(8,128)(2,1)} %param.12) | copy-start | bytes 589828
  3.6 0.9 %copy-start.3 = (f32[1,1,64,512]{3,2,1,0:T(8,128)S(1)}, f32[1,1,64,512]{3,2,1,0:T(8,128)}, u32[]{:S(2)}) copy-start(f32[1,1,64,512]{3,2,1,0:T(8,128)} %param.14) | copy-start | bytes 393220
  4.5 0.9 %copy-start.4 = (bf16[256,256]{1,0:T(8,128)(2,1)S(1)}, bf16[256,256]{1,0:T(8,128)(2,1)}, u32[]{:S(2)}) copy-start(bf16[256,256]{1,0:T(8,128)(2,1)} %constant.14.clone.bb_ref) | copy-start | bytes 393220
  5.4 0.9 %copy-start.5 = (bf16[256,256]{1,0:T(8,128)(2,1)S(1)}, bf16[256,256]{1,0:T(8,128)(2,1)}, u32[]{:S(2)}) copy-start(bf16[256,256]{1,0:T(8,128)(2,1)} %constant.12.clone.fh_ref) | copy-start | bytes 393220
  6.3 0.8 %copy-start.6 = (bf16[256,128]{1,0:T(8,128)(2,1)S(1)}, bf16[256,128]{1,0:T(8,128)(2,1)}, u32[]{:S(2)}) copy-start(bf16[256,128]{1,0:T(8,128)(2,1)} %constant.15.clone.bh_ref) | copy-start | bytes 196612
  7.2 0.8 %copy-start.7 = (bf16[128,256]{1,0:T(8,128)(2,1)S(1)}, bf16[128,256]{1,0:T(8,128)(2,1)}, u32[]{:S(2)}) copy-start(bf16[128,256]{1,0:T(8,128)(2,1)} %constant.13.clone.fl_ref) | copy-start | bytes 196612
  8.0 0.8 %copy-start.8 = (f32[64,128]{1,0:T(8,128)S(1)}, f32[64,128]{1,0:T(8,128)}, u32[]{:S(2)}) copy-start(f32[64,128]{1,0:T(8,128)} %constant.16.clone.coef_ref) | copy-start | bytes 98308
where the time goes:
time: 48.1 us; the launch traced here: 47.7 us
  Pallas kernels  38.1 us (79%)
  local copies, waits for them, and re-layouts  9.49 us (20%)
    pallas_call x1, Pallas kernels, local(): pl.pallas_call(functools.partial(kernel, nx, ny), out_shape=jax.ShapeDtyp...  38.1 us
    unnamed x23, local copies, waits for them, and re-layouts  9.49 us

commit v1 on v0

v1 whole, which is shorter than its diff:
```python
import functools

import jax
import jax.numpy as jnp
import numpy as np
from jax import lax
from jax.experimental import pallas as pl
from jax.experimental.pallas import tpu as pltpu
from jax.sharding import PartitionSpec as P

EX = 2
EY = 2
EZ = 16
ITERS = 4

time_step = 0.25
MESH = pl.DeviceIdType.MESH
f32 = jnp.float32
bf16 = jnp.bfloat16

SIDES = ((-1, 0), (1, 0), (0, -1), (0, 1))
CORNERS = ((-1, -1), (-1, 1), (1, -1), (1, 1))


def legendre_seven(points):
    previous = points * 0.0 + 1.0
    current = points
    for degree in range(1, 7):
        following = ((2 * degree + 1) * points * current - degree * previous) / (degree + 1)
        previous = current
        current = following
    return current


def gll_tables():
    poly_order = 7
    points = np.array(
        [
            -1.0,
            -0.8717401485096066,
            -0.5917001814331423,
            -0.2092992179024789,
            0.2092992179024789,
            0.5917001814331423,
            0.8717401485096066,
            1.0,
        ]
    )
    end_values = legendre_seven(points)
    weights = 2.0 / (poly_order * (poly_order + 1) * end_values**2)
    spread = points[:, None] - points[None, :]
    identity = np.eye(poly_order + 1)
    diff_table = end_values[:, None] / (end_values[None, :] * (spread + identity))
    diff_table = diff_table * (1.0 - identity)
    corners = np.zeros(poly_order + 1)
    corners[0] = -poly_order * (poly_order + 1) / 4.0
    corners[-1] = poly_order * (poly_order + 1) / 4.0
    diff_table = diff_table + identity * corners[None, :]
    return (weights.astype(np.float32), diff_table.astype(np.float32))


def constant_tables():
    weights, diff = gll_tables()
    eye = np.eye(8, dtype=np.float32)
    pair = np.eye(2, dtype=np.float32)
    along_j = np.kron(pair, np.kron(diff.T, eye))
    along_k = np.kron(pair, np.kron(eye, diff.T))
    coef = np.zeros((2, 2, 4, 4, 128), np.float32)
    for flip in range(2):
        matrix = diff.T if flip else diff
        for out in range(4):
            for inn in range(4):
                for il in range(2):
                    span = slice(il * 64, il * 64 + 64)
                    coef[flip, 0, out, inn, span] = matrix[2 * out + il, 2 * inn + il]
                    coef[flip, 1, out, inn, span] = matrix[2 * out + il, 2 * inn + 1 - il]
    coef = coef.reshape(64, 128)
    cube = weights[:, None, None] * weights[None, :, None] * weights[None, None, :]
    cube = np.concatenate([cube.reshape(4, 128), np.zeros((4, 128))])
    stack = [along_j, along_k, along_j.T, along_k.T, coef, cube]
    return np.concatenate(stack).astype(np.float32)


def dot(a, b):
    return jnp.dot(a, b, preferred_element_type=f32)


def split(values):
    high = values.astype(bf16)
    return high, (values - high.astype(f32)).astype(bf16)


def roll(values, shift, axis=None):
    axis = values.ndim - 1 if axis is None else axis
    shift = shift % values.shape[axis]
    return values if shift == 0 else pltpu.roll(values, shift, axis)


def kernel(
    nx,
    ny,
    adj_hbm,
    vel_hbm,
    dif_hbm,
    jac_hbm,
    slot_hbm,
    table_hbm,
    out_ref,
    adj_ref,
    vel_ref,
    dif_ref,
    jac_ref,
    slot_ref,
    table,
    forth,
    back,
    mass,
    cond,
    source,
    base0,
    base1,
    base2,
    base3,
    passed,
    dots,
    face_out,
    face_in,
    corner_out,
    corner_in,
    early_x,
    early_y,
    late,
    fetch_s,
    face_s,
    face_r,
    corner_s,
    corner_r,
    sums_s,
    sums_r,
):
    gx = lax.axis_index("gx")
    gy = lax.axis_index("gy")
    total = nx * ny
    me = gx * ny + gy
    cells = EX * EY * EZ

    fetches = [
        pltpu.make_async_copy(there, here, fetch_s.at[at])
        for at, (there, here) in enumerate(
            (
                (slot_hbm, slot_ref),
                (adj_hbm, adj_ref),
                (table_hbm, table),
                (jac_hbm, jac_ref),
                (vel_hbm, vel_ref),
                (dif_hbm, dif_ref),
            )
        )
    ]
    for fetch in fetches:
        fetch.start()
    got_slot, got_adj, got_table, got_jac, got_vel, got_dif = fetches

    face_in[...] = jnp.zeros_like(face_in)
    corner_in[...] = jnp.zeros_like(corner_in)

    barrier = pltpu.get_barrier_semaphore()

    def greet(step, carry):
        other = lax.rem(me + step, total)
        pl.semaphore_signal(
            barrier, inc=1, device_id=(other // ny, lax.rem(other, ny)), device_id_type=MESH
        )
        return carry

    lax.fori_loop(1, total, greet, 0)
    dots[...] = jnp.zeros_like(dots)

    lane = lax.broadcasted_iota(jnp.int32, (1, 128), 1)
    lane_j = (lane // 8) % 8
    lane_i = lane // 64
    group = lane // 8

    got_slot.wait()
    place = lax.broadcasted_iota(jnp.int32, (cells, cells), 0)
    picks = (jnp.broadcast_to(slot_ref[...], (cells, cells)) == place).astype(f32)
    pick = picks.astype(bf16)

    def thirds(values):
        high, low = split(values)
        return high, low, (values - high.astype(f32) - low.astype(f32)).astype(bf16)

    def to_brick(stored):
        high, low, last = thirds(stored)
        return dot(pick, high) + dot(pick, low) + dot(pick, last)

    def derive_jk(values):
        high, low = split(values)
        both = dot(jnp.concatenate([high, low], axis=1), forth[0:256, :])
        both = both + dot(high, forth[256:384, :])
        return both[:, :128], both[:, 128:]

    def derive_i(parts, flip):
        turned = [roll(part, 64) for part in parts]
        outs = []
        for out in range(4):
            acc = None
            for inn in range(4):
                at = 512 + flip * 32 + out * 4 + inn
                term = parts[inn] * table[at : at + 1, :]
                term = term + turned[inn] * table[at + 16 : at + 17, :]
                acc = term if acc is None else acc + term
            outs.append(acc)
        return outs

    def exists(side):
        ax, ay = gx + side[0], gy + side[1]
        return (ax >= 0) & (ax < nx) & (ay >= 0) & (ay < ny)

    def copies(turn, c):
        made = []
        groups = (
            (SIDES, face_out, face_in, face_s, face_r),
            (CORNERS, corner_out, corner_in, corner_s, corner_r),
        )
        for sides, outgoing, incoming, sent, received in groups:
            for d, side in enumerate(sides):
                copy = pltpu.make_async_remote_copy(
                    src_ref=outgoing.at[turn, c, d],
                    dst_ref=incoming.at[turn, c, d],
                    send_sem=sent.at[turn, c, d],
                    recv_sem=received.at[turn, c, d],
                    device_id=(gx + side[0], gy + side[1]),
                    device_id_type=MESH,
                )
                made.append((side, copy))
        return made

    def corner_spot(side):
        h = 0 if side[0] < 0 else 3
        x = 0 if side[0] < 0 else EX - 1
        y = 0 if side[1] < 0 else EY - 1
        start = (0 if side[0] < 0 else 64) + (0 if side[1] < 0 else 56)
        return h, x, y, start

    def fold_inside(values, dest, c):
        zed = lax.broadcasted_iota(jnp.int32, (EZ, 128), 0)
        kay = lax.broadcasted_iota(jnp.int32, (EZ, 128), 1) % 8
        upper = ((kay == 7) & (zed < EZ - 1)).astype(f32)
        lower = ((kay == 0) & (zed > 0)).astype(f32)
        flat = values.reshape(4 * cells, 128)
        stack = (4 * EX * EY, EZ, 128)
        from_next = roll(roll(flat, 7), -1, 0).reshape(stack)
        from_last = roll(roll(flat, -7), 1, 0).reshape(stack)
        summed = flat.reshape(stack) + from_next * upper[None] + from_last * lower[None]
        summed = summed.reshape(4, EX, EY, EZ, 128)
        columns = [summed[:, :, y] for y in range(EY)]
        folded = list(columns)
        for y in range(EY - 1):
            folded[y] = folded[y] + jnp.where(lane_j == 7, roll(columns[y + 1], 56), 0.0)
            folded[y + 1] = folded[y + 1] + jnp.where(lane_j == 0, roll(columns[y], -56), 0.0)
        for y in range(EY):
            dest[c, :, :, y] = folded[y]
        for x in range(EX - 1):
            left = dest[c, 3, x]
            right = dest[c, 0, x + 1]
            dest[c, 3, x] = left + jnp.where(lane_i == 1, roll(right, 64), 0.0)
            dest[c, 0, x + 1] = right + jnp.where(lane_i == 0, roll(left, 64), 0.0)

    def send_faces(turn, dest, c):
        left = dest[c, 0, 0]
        face_out[turn, c, 0] = jnp.where(lane_i == 0, left[0], roll(left[1], 64))
        right = dest[c, 3, EX - 1]
        face_out[turn, c, 1] = jnp.where(lane_i == 0, roll(right[0], 64), right[1])
        for d, y, j in ((2, 0, 0), (3, EY - 1, 7)):
            acc = None
            for h in range(4):
                for x in range(EX):
                    part = jnp.where(lane_j == j, dest[c, h, x, y], 0.0)
                    part = roll(part, h * 8 + x * 32 - j * 8)
                    acc = part if acc is None else acc + part
            face_out[turn, c, d] = acc
        for d, side in enumerate(CORNERS):
            h, x, y, start = corner_spot(side)
            corner_out[turn, c, d] = dest[c, h, x, y]
        for side, copy in copies(turn, c):
            pl.when(exists(side))(copy.start)

    def take_faces(turn, dest, c):
        for side, copy in copies(turn, c):
            pl.when(exists((-side[0], -side[1])))(copy.wait_recv)
        left = face_in[turn, c, 1]
        right = face_in[turn, c, 0]
        for h, x, arrived, here in ((0, 0, left, 0), (3, EX - 1, right, 1)):
            turned = roll(arrived, 64)
            pair = (arrived, turned) if here == 0 else (turned, arrived)
            for y in range(EY):
                dest[c, h, x, y] = dest[c, h, x, y] + jnp.where(lane_i == here, pair[y], 0.0)
        for d, y, j in ((3, 0, 0), (2, EY - 1, 7)):
            arrived = face_in[turn, c, d]
            for h in range(4):
                for x in range(EX):
                    part = roll(arrived, j * 8 - h * 8 - x * 32)
                    dest[c, h, x, y] = dest[c, h, x, y] + jnp.where(lane_j == j, part, 0.0)
        for d, side in enumerate(CORNERS):
            h, x, y, start = corner_spot((-side[0], -side[1]))
            other = corner_spot(side)[3]
            part = roll(corner_in[turn, c, d], start - other)
            dest[c, h, x, y] = dest[c, h, x, y] + jnp.where(group == start // 8, part, 0.0)

    def operate(values):
        grad_j, grad_k = derive_jk(values.reshape(4 * cells, 128))
        flux_j = grad_j * cond[1].reshape(4 * cells, 128)
        flux_k = grad_k * cond[2].reshape(4 * cells, 128)
        high, low = split(jnp.concatenate([flux_j, flux_k], axis=1))
        both = dot(high, back[...])
        stiff = both[:, :128] + both[:, 128:] + dot(low, back[:, 0:128])
        stiff = stiff.reshape(4, cells, 128)
        grads = derive_i([values[h] for h in range(4)], 0)
        fluxes = [grads[h] * cond[0, h] for h in range(4)]
        backs = derive_i(fluxes, 1)
        return [mass[h] * values[h] + stiff[h] + backs[h] for h in range(4)]

    def load(ref, c):
        return ref[c].reshape(4, cells, 128)

    def add_dot(at, first, second):
        acc = dots[at]
        for h in range(4):
            acc = acc + jnp.sum((first[h] * second[h]).reshape(cells // 8, 8, 128), axis=0)
        dots[at] = acc

    def in_row(first, last):
        sums = jnp.sum(jnp.sum(dots[first:last], axis=1), axis=1, keepdims=True)
        spot = lax.broadcasted_iota(jnp.int32, (last - first, 128), 0)
        here = lax.broadcasted_iota(jnp.int32, (last - first, 128), 1)
        return jnp.sum(jnp.where(spot == here, sums, 0.0), axis=0, keepdims=True)

    def spread_sums(buffer, at, spot, count, device):
        buffer[spot] = buffer_row[0]

        def send(step, carry):
            pltpu.make_async_remote_copy(
                src_ref=buffer.at[spot],
                dst_ref=buffer.at[spot],
                send_sem=sums_s.at[at],
                recv_sem=sums_r.at[at],
                device_id=device(step),
                device_id_type=MESH,
            ).start()
            return carry

        lax.fori_loop(1, count, send, 0)

    def await_sums(buffer, at, count, sems):
        arrived = buffer.at[pl.ds(0, count - 1)]
        pltpu.make_async_copy(arrived, arrived, sems.at[at]).wait()

    buffer_row = [None]

    def along_x(step):
        return lax.rem(gx + step, nx), gy

    def along_y(step):
        return gx, lax.rem(gy + step, ny)

    def anywhere(step):
        other = lax.rem(me + step, total)
        return other // ny, lax.rem(other, ny)

    got_adj.wait()
    adj = [to_brick(adj_ref[c]) for c in range(3)]
    got_table.wait()
    f_high, f_low = split(jnp.concatenate([table[0:128], table[128:256]], axis=1))
    forth[0:128, :] = f_high
    forth[128:256, :] = f_high
    forth[256:384, :] = f_low
    b_high, b_low = split(table[256:512])
    back[...] = jnp.concatenate([b_high, b_low], axis=1)
    got_jac.wait()
    jac = to_brick(jac_ref[0])
    for h in range(4):
        mass[h] = jac[:, h * 128 : h * 128 + 128] * table[576 + h : 577 + h, :]
    full = [[adj[c][:, h * 128 : h * 128 + 128] for h in range(4)] for c in range(3)]
    grad_j, grad_k, grad_i = [], [], []
    for c in range(3):
        g_j, g_k = derive_jk(jnp.concatenate(full[c], axis=0))
        grad_j.append(g_j.reshape(4, cells, 128))
        grad_k.append(g_k.reshape(4, cells, 128))
        grad_i.append(derive_i(full[c], 0))
    got_vel.wait()
    flow = [dot(pick, vel_ref[c]) for c in range(3)]
    for h in range(4):
        at = slice(h * 128, h * 128 + 128)
        v = [flow[c][:, at] for c in range(3)]
        r = [
            grad_j[2][h] - grad_k[1][h],
            grad_k[0][h] - grad_i[2][h],
            grad_i[1][h] - grad_j[0][h],
        ]
        for c in range(3):
            c1, c2 = (c + 1) % 3, (c + 2) % 3
            value = full[c][h] + time_step * (v[c1] * r[c2] - v[c2] * r[c1])
            source[c, h] = mass[h] * value

    pl.semaphore_wait(barrier, total - 1)

    def first_send(c, carry):
        fold_inside(source[c], base0, c)
        send_faces(0, base0, c)
        return carry

    lax.fori_loop(0, 3, first_send, 0)

    got_dif.wait()
    for m in range(3):
        con = to_brick(dif_ref[m])
        for h in range(4):
            weight = time_step * table[576 + h : 577 + h, :]
            cond[m, h] = con[:, h * 128 : h * 128 + 128] * weight

    def turn_0(c, carry):
        take_faces(0, base0, c)
        values = load(base0, c)
        add_dot(0, values, source[c])
        applied = operate(values)
        add_dot(1, values, applied)
        fold_inside(jnp.stack(applied), base1, c)
        send_faces(1, base1, c)
        return carry

    lax.fori_loop(0, 3, turn_0, 0)
    buffer_row[0] = in_row(0, 8)
    spread_sums(early_x, 0, gx, nx, along_x)

    def turn_1(c, carry):
        @pl.when(c == 1)
        def _():
            await_sums(early_x, 0, nx, sums_r)
            buffer_row[0] = jnp.sum(early_x[...], axis=0)
            spread_sums(early_y, 1, gy, ny, along_y)

        take_faces(1, base1, c)
        values = load(base1, c)
        applied = operate(values)
        add_dot(8, load(base0, c), applied)
        add_dot(9, values, applied)
        fold_inside(jnp.stack(applied), passed, c)
        send_faces(2, passed, c)
        return carry

    lax.fori_loop(0, 3, turn_1, 0)
    await_sums(early_y, 1, ny, sums_r)
    early = jnp.sum(early_y[...], axis=0)
    norm = early[:, 0:1]
    first = early[:, 1:2]
    inv = norm / (1.75 * first)

    def turn_2(c, carry):
        take_faces(2, passed, c)
        u0, u1, q = load(base0, c), load(base1, c), load(passed, c)
        v1 = inv * u1 - u0
        values = 2.0 * (inv * (inv * q - u1) - v1) - u0
        base2[c] = values
        applied = operate(values)
        add_dot(10, u0, applied)
        add_dot(11, u1, applied)
        add_dot(12, values, applied)
        fold_inside(jnp.stack(applied), passed, c)
        send_faces(3, passed, c)
        return carry

    lax.fori_loop(0, 3, turn_2, 0)

    def turn_3(c, carry):
        take_faces(3, passed, c)
        u0, u1, v2, q = load(base0, c), load(base1, c), base2[c], load(passed, c)
        values = 2.0 * (inv * q - v2) - (inv * u1 - u0)
        base3[c] = values
        applied = operate(values)
        add_dot(13, u0, applied)
        add_dot(14, u1, applied)
        add_dot(15, v2, applied)
        add_dot(16, values, applied)
        return carry

    lax.fori_loop(0, 3, turn_3, 0)
    buffer_row[0] = in_row(8, 24)
    spread_sums(late, 2, me, total, anywhere)

    def drain(at, carry):
        for side, copy in copies(at // 3, at % 3):
            pl.when(exists(side))(copy.wait_send)
        return carry

    lax.fori_loop(0, 3 * ITERS, drain, 0)
    await_sums(early_x, 0, nx, sums_s)
    await_sums(early_y, 1, ny, sums_s)

    await_sums(late, 2, total, sums_r)
    row = jnp.sum(late[...], axis=0)
    d = [row[:, at : at + 1] for at in range(9)]
    a = inv * first
    g2 = 2.0 * inv * inv * d[0] - 4.0 * a + norm
    g3 = 2.0 * (inv * d[2] - g2) - (a - norm)
    gram = [
        [first, d[0], d[2], d[5]],
        [d[0], d[1], d[3], d[6]],
        [d[2], d[3], d[4], d[7]],
        [d[5], d[6], d[7], d[8]],
    ]
    side = [norm, first, g2, g3]
    diagonal = [gram[at][at] for at in range(4)]
    inverse = []
    for at in range(4):
        pivot = gram[at][at]
        usable = pivot > 1e-6 * diagonal[at]
        inverse.append(jnp.where(usable, 1.0 / pivot, 0.0))
        for below in range(at + 1, 4):
            factor = gram[below][at] * inverse[at]
            for across in range(at + 1, 4):
                gram[below][across] = gram[below][across] - factor * gram[at][across]
            side[below] = side[below] - factor * side[at]
    weights = [None] * 4
    for at in (3, 2, 1, 0):
        value = side[at]
        for across in range(at + 1, 4):
            value = value - gram[at][across] * weights[across]
        weights[at] = value * inverse[at]

    put_back = picks.T.astype(bf16)
    for c in range(3):
        mixed = weights[0] * load(base0, c) + weights[1] * load(base1, c)
        mixed = mixed + weights[2] * base2[c] + weights[3] * base3[c]
        whole = jnp.concatenate([mixed[h] for h in range(4)], axis=1)
        high, low, last = thirds(whole)
        out_ref[c] = dot(put_back, high) + dot(put_back, low) + dot(put_back, last)
    await_sums(late, 2, total, sums_s)


def local(nx, ny, adjoint_field, velocity, diffusivity, jacobian, element_slot):
    table = jnp.asarray(constant_tables())
    cells = element_slot.size
    nodes = adjoint_field.shape[-1]
    brick = (3, 4, EX, EY, EZ, 128)
    flat = (3, 4, cells, 128)
    hbm = pl.BlockSpec(memory_space=pltpu.HBM)
    result = pl.pallas_call(
        functools.partial(kernel, nx, ny),
        out_shape=jax.ShapeDtypeStruct((3, cells, nodes), f32),
        in_specs=[hbm] * 6,
        out_specs=pl.BlockSpec(memory_space=pltpu.VMEM),
        scratch_shapes=[
            pltpu.VMEM((3, cells, nodes), f32),
            pltpu.VMEM((3, cells, nodes), bf16),
            pltpu.VMEM((3, cells, nodes), f32),
            pltpu.VMEM((1, cells, nodes), f32),
            pltpu.VMEM((1, cells), jnp.int32),
            pltpu.VMEM(table.shape, f32),
            pltpu.VMEM((384, 256), bf16),
            pltpu.VMEM((256, 256), bf16),
            pltpu.VMEM((4, cells, 128), f32),
            pltpu.VMEM(flat, f32),
            pltpu.VMEM(flat, f32),
            pltpu.VMEM(brick, f32),
            pltpu.VMEM(brick, f32),
            pltpu.VMEM(flat, f32),
            pltpu.VMEM(flat, f32),
            pltpu.VMEM(brick, f32),
            pltpu.VMEM((24, 8, 128), f32),
            pltpu.VMEM((ITERS, 3, 4, EZ, 128), f32),
            pltpu.VMEM((ITERS, 3, 4, EZ, 128), f32),
            pltpu.VMEM((ITERS, 3, 4, EZ, 128), f32),
            pltpu.VMEM((ITERS, 3, 4, EZ, 128), f32),
            pltpu.VMEM((nx, 1, 128), f32),
            pltpu.VMEM((ny, 1, 128), f32),
            pltpu.VMEM((nx * ny, 1, 128), f32),
            pltpu.SemaphoreType.DMA((6,)),
            pltpu.SemaphoreType.DMA((ITERS, 3, 4)),
            pltpu.SemaphoreType.DMA((ITERS, 3, 4)),
            pltpu.SemaphoreType.DMA((ITERS, 3, 4)),
            pltpu.SemaphoreType.DMA((ITERS, 3, 4)),
            pltpu.SemaphoreType.DMA((3,)),
            pltpu.SemaphoreType.DMA((3,)),
        ],
        compiler_params=pltpu.CompilerParams(
            collective_id=0, has_side_effects=True, vmem_limit_bytes=48 * 1024 * 1024
        ),
    )(
        adjoint_field.reshape(3, cells, nodes),
        velocity.reshape(3, cells, nodes),
        diffusivity.reshape(3, cells, nodes),
        jacobian.reshape(1, cells, nodes),
        element_slot.reshape(1, cells),
        table,
    )
    return result.reshape(3, 1, 1, cells, nodes)


def solution(mesh):
    in_specs = (
        P(None, "gx", "gy", None, None),
        P(None, "gx", "gy", None, None),
        P(None, "gx", "gy", None, None),
        P("gx", "gy", None, None),
        P("gx", "gy", None),
    )
    out_specs = P(None, "gx", "gy", None, None)
    run = functools.partial(local, mesh.shape["gx"], mesh.shape["gy"])
    return jax.shard_map(run, mesh=mesh, in_specs=in_specs, out_specs=out_specs, check_vma=False)
```

time: 48.1 us -> 41.4 us (0.86)
  local copies, waits for them, and re-layouts: 9.49 us -> 6.19 us
  Pallas kernels: 38.1 us -> 35 us
    unnamed x23 -> x13, local copies, waits for them, and re-layouts: 9.49 us -> 6.19 us
    pallas_call x1, Pallas kernels: 38.1 us -> 35 us  [local(): pl.pallas_call(functools.partial(kernel, nx, ny), out_shape=jax.ShapeDtyp...]
where the time goes in v1:
time: 41.4 us; the launch traced here: 41.2 us
  Pallas kernels  35 us (85%)
  local copies, waits for them, and re-layouts  6.19 us (15%)
    pallas_call x1, Pallas kernels, local(): pl.pallas_call(functools.partial(kernel, nx, ny), out_shape=jax.ShapeDtyp...  35 us
    unnamed x13, local copies, waits for them, and re-layouts  6.19 us

profile of v1, /device:TPU:0, one launch (start us, length us, event | category | flops | bytes accessed | tf_op | source)
XLA Modules:
  0.0 41.2 jit_solution(5622585301149840324)
XLA Ops:
  0.0 0.0 copy-start.5
  0.0 0.7 %copy-done.5 = s32[1,1,64]{2,1,0:T(1,128)S(1)} copy-done((s32[1,1,64]{2,1,0:T(1,128)S(1)}, s32[1,1,64]{2,1,0:T(1,128)}, u32[]{:S(2)}) %copy-start.5) | copy-done | bytes 280
  0.7 0.0 copy-start
  0.7 1.0 %copy-done = f32[3,1,1,64,512]{4,3,2,1,0:T(8,128)S(1)} copy-done((f32[3,1,1,64,512]{4,3,2,1,0:T(8,128)S(1)}, f32[3,1,1,64,512]{4,3,2,1,0:T(8,128)}, u32[]{:S(2)}) %copy-start) | copy-done | bytes 393240
  1.7 0.0 copy-start.1
  1.7 1.0 %copy-done.1 = f32[3,1,1,64,512]{4,3,2,1,0:T(8,128)S(1)} copy-done((f32[3,1,1,64,512]{4,3,2,1,0:T(8,128)S(1)}, f32[3,1,1,64,512]{4,3,2,1,0:T(8,128)}, u32[]{:S(2)}) %copy-start.1) | copy-done | bytes 393240
  2.6 0.0 copy-start.2
  2.7 1.0 %copy-done.2 = f32[584,128]{1,0:T(8,128)S(1)} copy-done((f32[584,128]{1,0:T(8,128)S(1)}, f32[584,128]{1,0:T(8,128)}, u32[]{:S(2)}) %copy-start.2) | copy-done | bytes 299032
  3.6 0.0 copy-start.3
  3.6 0.9 %copy-done.3 = bf16[3,1,1,64,512]{4,3,2,1,0:T(8,128)(2,1)S(1)} copy-done((bf16[3,1,1,64,512]{4,3,2,1,0:T(8,128)(2,1)S(1)}, bf16[3,1,1,64,512]{4,3,2,1,0:T(8,128)(2,1)}, u32[]{:S(2)}) %copy-start.3) | copy-done | bytes 196632
  4.5 0.0 copy-start.4
  4.5 0.9 %copy-done.4 = f32[1,1,64,512]{3,2,1,0:T(8,128)S(1)} copy-done((f32[1,1,64,512]{3,2,1,0:T(8,128)S(1)}, f32[1,1,64,512]{3,2,1,0:T(8,128)}, u32[]{:S(2)}) %copy-start.4) | copy-done | bytes 131096
  5.4 35.0 %shard_map.64 = f32[3,64,512]{2,1,0:T(8,128)S(1)} custom-call(f32[3,64,512]{2,1,0:T(8,128)S(1)} %bitcast.9, bf16[3,64,512]{2,1,0:T(8,128)(2,1)S(1)} %bitcast.11, f32[3,64,512]{2,1,0:T(8,128)S(1)} %bitcast.10, f32[1,64,512]{2,1,0:T(8,128)S(1)} %bitcast.12, s32[1,64]{1,0:T(1,128)S(1)} %bitcast.13, f32[584,128]{1,0:T(8,128)S(1)} %copy-done.2), custom_call_target="tpu_custom_call" | custom-call | tf_op jit(solution)/shard_map/pallas_call | solution.py:548
  40.4 0.7 %copy.9 = f32[3,1,1,64,512]{4,3,2,1,0:T(8,128)} copy(f32[3,1,1,64,512]{4,3,2,1,0:T(8,128)S(1)} %bitcast.8) | data formatting | bytes 786432
Async XLA Ops:
  0.0 0.7 %copy-start.5 = (s32[1,1,64]{2,1,0:T(1,128)S(1)}, s32[1,1,64]{2,1,0:T(1,128)}, u32[]{:S(2)}) copy-start(s32[1,1,64]{2,1,0:T(1,128)} %param.10) | copy-start | bytes 772
  0.7 1.0 %copy-start = (f32[3,1,1,64,512]{4,3,2,1,0:T(8,128)S(1)}, f32[3,1,1,64,512]{4,3,2,1,0:T(8,128)}, u32[]{:S(2)}) copy-start(f32[3,1,1,64,512]{4,3,2,1,0:T(8,128)} %param.6) | copy-start | bytes 1179652
  1.7 1.0 %copy-start.1 = (f32[3,1,1,64,512]{4,3,2,1,0:T(8,128)S(1)}, f32[3,1,1,64,512]{4,3,2,1,0:T(8,128)}, u32[]{:S(2)}) copy-start(f32[3,1,1,64,512]{4,3,2,1,0:T(8,128)} %param.8) | copy-start | bytes 1179652
  2.6 1.0 %copy-start.2 = (f32[584,128]{1,0:T(8,128)S(1)}, f32[584,128]{1,0:T(8,128)}, u32[]{:S(2)}) copy-start(f32[584,128]{1,0:T(8,128)} %constant.2.clone.table_hbm) | copy-start | bytes 897028
  3.6 0.9 %copy-start.3 = (bf16[3,1,1,64,512]{4,3,2,1,0:T(8,128)(2,1)S(1)}, bf16[3,1,1,64,512]{4,3,2,1,0:T(8,128)(2,1)}, u32[]{:S(2)}) copy-start(bf16[3,1,1,64,512]{4,3,2,1,0:T(8,128)(2,1)} %param.7) | copy-start | bytes 589828
  4.5 0.9 %copy-start.4 = (f32[1,1,64,512]{3,2,1,0:T(8,128)S(1)}, f32[1,1,64,512]{3,2,1,0:T(8,128)}, u32[]{:S(2)}) copy-start(f32[1,1,64,512]{3,2,1,0:T(8,128)} %param.9) | copy-start | bytes 393220

commit v2 on v1

--- a/solution.py
+++ b/solution.py
@@ -186,13 +186,10 @@
     picks = (jnp.broadcast_to(slot_ref[...], (cells, cells)) == place).astype(f32)
     pick = picks.astype(bf16)
 
-    def thirds(values):
-        high, low = split(values)
-        return high, low, (values - high.astype(f32) - low.astype(f32)).astype(bf16)
+    pick_both = jnp.concatenate([pick, pick], axis=1)
 
     def to_brick(stored):
-        high, low, last = thirds(stored)
-        return dot(pick, high) + dot(pick, low) + dot(pick, last)
+        return dot(pick_both, jnp.concatenate(split(stored), axis=0))
 
     def derive_jk(values):
         high, low = split(values)
@@ -336,8 +333,8 @@
         here = lax.broadcasted_iota(jnp.int32, (last - first, 128), 1)
         return jnp.sum(jnp.where(spot == here, sums, 0.0), axis=0, keepdims=True)
 
-    def spread_sums(buffer, at, spot, count, device):
-        buffer[spot] = buffer_row[0]
+    def spread_sums(row, buffer, at, spot, count, device):
+        buffer[spot] = row
 
         def send(step, carry):
             pltpu.make_async_remote_copy(
@@ -355,8 +352,6 @@
     def await_sums(buffer, at, count, sems):
         arrived = buffer.at[pl.ds(0, count - 1)]
         pltpu.make_async_copy(arrived, arrived, sems.at[at]).wait()
-
-    buffer_row = [None]
 
     def along_x(step):
         return lax.rem(gx + step, nx), gy
@@ -430,15 +425,13 @@
         return carry
 
     lax.fori_loop(0, 3, turn_0, 0)
-    buffer_row[0] = in_row(0, 8)
-    spread_sums(early_x, 0, gx, nx, along_x)
+    spread_sums(in_row(0, 8), early_x, 0, gx, nx, along_x)
 
     def turn_1(c, carry):
         @pl.when(c == 1)
         def _():
             await_sums(early_x, 0, nx, sums_r)
-            buffer_row[0] = jnp.sum(early_x[...], axis=0)
-            spread_sums(early_y, 1, gy, ny, along_y)
+            spread_sums(jnp.sum(early_x[...], axis=0), early_y, 1, gy, ny, along_y)
 
         take_faces(1, base1, c)
         values = load(base1, c)
@@ -485,8 +478,7 @@
         return carry
 
     lax.fori_loop(0, 3, turn_3, 0)
-    buffer_row[0] = in_row(8, 24)
-    spread_sums(late, 2, me, total, anywhere)
+    spread_sums(in_row(8, 24), late, 2, me, total, anywhere)
 
     def drain(at, carry):
         for side, copy in copies(at // 3, at % 3):
@@ -529,12 +521,12 @@
         weights[at] = value * inverse[at]
 
     put_back = picks.T.astype(bf16)
+    put_back = jnp.concatenate([put_back, put_back], axis=1)
     for c in range(3):
         mixed = weights[0] * load(base0, c) + weights[1] * load(base1, c)
         mixed = mixed + weights[2] * base2[c] + weights[3] * base3[c]
         whole = jnp.concatenate([mixed[h] for h in range(4)], axis=1)
-        high, low, last = thirds(whole)
-        out_ref[c] = dot(put_back, high) + dot(put_back, low) + dot(put_back, last)
+        out_ref[c] = dot(put_back, jnp.concatenate(split(whole), axis=0))
     await_sums(late, 2, total, sums_s)
 
 
@@ -584,7 +576,7 @@
             pltpu.SemaphoreType.DMA((3,)),
         ],
         compiler_params=pltpu.CompilerParams(
-            collective_id=0, has_side_effects=True, vmem_limit_bytes=48 * 1024 * 1024
+            collective_id=0, has_side_effects=True
         ),
     )(
         adjoint_field.reshape(3, cells, nodes),

time: 41.4 us -> 36.7 us (0.89)
  local copies, waits for them, and re-layouts: 6.19 us -> 1.77 us
    unnamed x13 -> x1, local copies, waits for them, and re-layouts: 6.19 us -> 1.77 us
where the time goes in v2:
time: 36.7 us; the launch traced here: 36.6 us
  Pallas kernels  34.8 us (95%)
  local copies, waits for them, and re-layouts  1.77 us (5%)
    pallas_call x1, Pallas kernels, local(): pl.pallas_call(functools.partial(kernel, nx, ny), out_shape=jax.ShapeDtyp...  34.8 us
    unnamed x1, local copies, waits for them, and re-layouts  1.77 us

profile of v2, /device:TPU:0, one launch (start us, length us, event | category | flops | bytes accessed | tf_op | source)
XLA Modules:
  0.0 36.6 jit_solution(15395102228819689084)
XLA Ops:
  0.0 34.8 %shard_map.64 = f32[3,64,512]{2,1,0:T(8,128)} custom-call(f32[3,64,512]{2,1,0:T(8,128)} %bitcast.9, bf16[3,64,512]{2,1,0:T(8,128)(2,1)} %bitcast.11, f32[3,64,512]{2,1,0:T(8,128)} %bitcast.10, f32[1,64,512]{2,1,0:T(8,128)} %bitcast.12, s32[1,64]{1,0:T(1,128)} %bitcast.13, f32[584,128]{1,0:T(8,128)} %constant.2.clone.table_hbm), custom_call_target="tpu_custom_call" | custom-call | tf_op jit(solution)/shard_map/pallas_call | solution.py:540
  34.8 1.8 %copy.9 = f32[3,1,1,64,512]{4,3,2,1,0:T(8,128)} copy(f32[3,1,1,64,512]{4,3,2,1,0:T(8,128)} %bitcast.8) | data formatting | bytes 786432

commit v3 on v2

--- a/solution.py
+++ b/solution.py
@@ -19,7 +19,6 @@
 bf16 = jnp.bfloat16
 
 SIDES = ((-1, 0), (1, 0), (0, -1), (0, 1))
-CORNERS = ((-1, -1), (-1, 1), (1, -1), (1, 1))
 
 
 def legendre_seven(points):
@@ -117,24 +116,18 @@
     mass,
     cond,
     source,
-    base0,
-    base1,
+    field,
     base2,
     base3,
-    passed,
     dots,
     face_out,
     face_in,
-    corner_out,
-    corner_in,
     early_x,
     early_y,
     late,
     fetch_s,
     face_s,
     face_r,
-    corner_s,
-    corner_r,
     sums_s,
     sums_r,
 ):
@@ -162,7 +155,6 @@
     got_slot, got_adj, got_table, got_jac, got_vel, got_dif = fetches
 
     face_in[...] = jnp.zeros_like(face_in)
-    corner_in[...] = jnp.zeros_like(corner_in)
 
     barrier = pltpu.get_barrier_semaphore()
 
@@ -179,7 +171,6 @@
     lane = lax.broadcasted_iota(jnp.int32, (1, 128), 1)
     lane_j = (lane // 8) % 8
     lane_i = lane // 64
-    group = lane // 8
 
     got_slot.wait()
     place = lax.broadcasted_iota(jnp.int32, (cells, cells), 0)
@@ -214,33 +205,31 @@
         ax, ay = gx + side[0], gy + side[1]
         return (ax >= 0) & (ax < nx) & (ay >= 0) & (ay < ny)
 
-    def copies(turn, c):
+    def copies(turn, c, sides):
         made = []
-        groups = (
-            (SIDES, face_out, face_in, face_s, face_r),
-            (CORNERS, corner_out, corner_in, corner_s, corner_r),
-        )
-        for sides, outgoing, incoming, sent, received in groups:
-            for d, side in enumerate(sides):
+        for d, side in enumerate(SIDES):
+            if side in sides:
                 copy = pltpu.make_async_remote_copy(
-                    src_ref=outgoing.at[turn, c, d],
-                    dst_ref=incoming.at[turn, c, d],
-                    send_sem=sent.at[turn, c, d],
-                    recv_sem=received.at[turn, c, d],
+                    src_ref=face_out.at[turn, c, d],
+                    dst_ref=face_in.at[turn, c, d],
+                    send_sem=face_s.at[turn, c, d],
+                    recv_sem=face_r.at[turn, c, d],
                     device_id=(gx + side[0], gy + side[1]),
                     device_id_type=MESH,
                 )
                 made.append((side, copy))
         return made
 
-    def corner_spot(side):
-        h = 0 if side[0] < 0 else 3
-        x = 0 if side[0] < 0 else EX - 1
-        y = 0 if side[1] < 0 else EY - 1
-        start = (0 if side[0] < 0 else 64) + (0 if side[1] < 0 else 56)
-        return h, x, y, start
-
-    def fold_inside(values, dest, c):
+    def start(turn, c, sides):
+        for side, copy in copies(turn, c, sides):
+            pl.when(exists(side))(copy.start)
+
+    def await_faces(turn, c, sides):
+        for side, copy in copies(turn, c, sides):
+            pl.when(exists((-side[0], -side[1])))(copy.wait_recv)
+
+    def fold_inside(values, turn, c):
+        dest = field.at[turn]
         zed = lax.broadcasted_iota(jnp.int32, (EZ, 128), 0)
         kay = lax.broadcasted_iota(jnp.int32, (EZ, 128), 1) % 8
         upper = ((kay == 7) & (zed < EZ - 1)).astype(f32)
@@ -264,46 +253,46 @@
             dest[c, 3, x] = left + jnp.where(lane_i == 1, roll(right, 64), 0.0)
             dest[c, 0, x + 1] = right + jnp.where(lane_i == 0, roll(left, 64), 0.0)
 
-    def send_faces(turn, dest, c):
-        left = dest[c, 0, 0]
+    def send_x(turn, c):
+        left = field[turn, c, 0, 0]
         face_out[turn, c, 0] = jnp.where(lane_i == 0, left[0], roll(left[1], 64))
-        right = dest[c, 3, EX - 1]
+        right = field[turn, c, 3, EX - 1]
         face_out[turn, c, 1] = jnp.where(lane_i == 0, roll(right[0], 64), right[1])
-        for d, y, j in ((2, 0, 0), (3, EY - 1, 7)):
-            acc = None
-            for h in range(4):
-                for x in range(EX):
-                    part = jnp.where(lane_j == j, dest[c, h, x, y], 0.0)
-                    part = roll(part, h * 8 + x * 32 - j * 8)
-                    acc = part if acc is None else acc + part
-            face_out[turn, c, d] = acc
-        for d, side in enumerate(CORNERS):
-            h, x, y, start = corner_spot(side)
-            corner_out[turn, c, d] = dest[c, h, x, y]
-        for side, copy in copies(turn, c):
-            pl.when(exists(side))(copy.start)
-
-    def take_faces(turn, dest, c):
-        for side, copy in copies(turn, c):
-            pl.when(exists((-side[0], -side[1])))(copy.wait_recv)
+        start(turn, c, SIDES[:2])
+
+    def pass_on(turn, c):
+        await_faces(turn, c, SIDES[:2])
         left = face_in[turn, c, 1]
         right = face_in[turn, c, 0]
         for h, x, arrived, here in ((0, 0, left, 0), (3, EX - 1, right, 1)):
             turned = roll(arrived, 64)
             pair = (arrived, turned) if here == 0 else (turned, arrived)
             for y in range(EY):
-                dest[c, h, x, y] = dest[c, h, x, y] + jnp.where(lane_i == here, pair[y], 0.0)
+                values = field[turn, c, h, x, y]
+                field[turn, c, h, x, y] = values + jnp.where(lane_i == here, pair[y], 0.0)
+        for d, y, j in ((2, 0, 0), (3, EY - 1, 7)):
+            acc = None
+            for h in range(4):
+                for x in range(EX):
+                    part = jnp.where(lane_j == j, field[turn, c, h, x, y], 0.0)
+                    part = roll(part, h * 8 + x * 32 - j * 8)
+                    acc = part if acc is None else acc + part
+            face_out[turn, c, d] = acc
+        start(turn, c, SIDES[2:])
+
+    def take_y(turn, c):
+        await_faces(turn, c, SIDES[2:])
         for d, y, j in ((3, 0, 0), (2, EY - 1, 7)):
             arrived = face_in[turn, c, d]
             for h in range(4):
                 for x in range(EX):
                     part = roll(arrived, j * 8 - h * 8 - x * 32)
-                    dest[c, h, x, y] = dest[c, h, x, y] + jnp.where(lane_j == j, part, 0.0)
-        for d, side in enumerate(CORNERS):
-            h, x, y, start = corner_spot((-side[0], -side[1]))
-            other = corner_spot(side)[3]
-            part = roll(corner_in[turn, c, d], start - other)
-            dest[c, h, x, y] = dest[c, h, x, y] + jnp.where(group == start // 8, part, 0.0)
+                    values = field[turn, c, h, x, y]
+                    field[turn, c, h, x, y] = values + jnp.where(lane_j == j, part, 0.0)
+
+    def pass_previous(turn, c):
+        before = 3 * turn + c + 2
+        pass_on(before // 3, lax.rem(before, 3))
 
     def operate(values):
         grad_j, grad_k = derive_jk(values.reshape(4 * cells, 128))
@@ -318,8 +307,8 @@
         backs = derive_i(fluxes, 1)
         return [mass[h] * values[h] + stiff[h] + backs[h] for h in range(4)]
 
-    def load(ref, c):
-        return ref[c].reshape(4, cells, 128)
+    def load(turn, c):
+        return field[turn, c].reshape(4, cells, 128)
 
     def add_dot(at, first, second):
         acc = dots[at]
@@ -401,11 +390,13 @@
     pl.semaphore_wait(barrier, total - 1)
 
     def first_send(c, carry):
-        fold_inside(source[c], base0, c)
-        send_faces(0, base0, c)
+        fold_inside(source[c], 0, c)
+        send_x(0, c)
         return carry
 
     lax.fori_loop(0, 3, first_send, 0)
+    pass_on(0, 0)
+    pass_on(0, 1)
 
     got_dif.wait()
     for m in range(3):
@@ -414,14 +405,17 @@
             weight = time_step * table[576 + h : 577 + h, :]
             cond[m, h] = con[:, h * 128 : h * 128 + 128] * weight
 
+    pass_on(0, 2)
+
     def turn_0(c, carry):
-        take_faces(0, base0, c)
-        values = load(base0, c)
+        take_y(0, c)
+        values = load(0, c)
         add_dot(0, values, source[c])
         applied = operate(values)
         add_dot(1, values, applied)
-        fold_inside(jnp.stack(applied), base1, c)
-        send_faces(1, base1, c)
+        pl.when(c > 0)(lambda: pass_on(1, c - 1))
+        fold_inside(jnp.stack(applied), 1, c)
+        send_x(1, c)
         return carry
 
     lax.fori_loop(0, 3, turn_0, 0)
@@ -433,13 +427,14 @@
             await_sums(early_x, 0, nx, sums_r)
             spread_sums(jnp.sum(early_x[...], axis=0), early_y, 1, gy, ny, along_y)
 
-        take_faces(1, base1, c)
-        values = load(base1, c)
+        take_y(1, c)
+        values = load(1, c)
         applied = operate(values)
-        add_dot(8, load(base0, c), applied)
+        add_dot(8, load(0, c), applied)
         add_dot(9, values, applied)
-        fold_inside(jnp.stack(applied), passed, c)
-        send_faces(2, passed, c)
+        pass_previous(1, c)
+        fold_inside(jnp.stack(applied), 2, c)
+        send_x(2, c)
         return carry
 
     lax.fori_loop(0, 3, turn_1, 0)
@@ -450,8 +445,8 @@
     inv = norm / (1.75 * first)
 
     def turn_2(c, carry):
-        take_faces(2, passed, c)
-        u0, u1, q = load(base0, c), load(base1, c), load(passed, c)
+        take_y(2, c)
+        u0, u1, q = load(0, c), load(1, c), load(2, c)
         v1 = inv * u1 - u0
         values = 2.0 * (inv * (inv * q - u1) - v1) - u0
         base2[c] = values
@@ -459,15 +454,16 @@
         add_dot(10, u0, applied)
         add_dot(11, u1, applied)
         add_dot(12, values, applied)
-        fold_inside(jnp.stack(applied), passed, c)
-        send_faces(3, passed, c)
+        pass_previous(2, c)
+        fold_inside(jnp.stack(applied), 3, c)
+        send_x(3, c)
         return carry
 
     lax.fori_loop(0, 3, turn_2, 0)
 
     def turn_3(c, carry):
-        take_faces(3, passed, c)
-        u0, u1, v2, q = load(base0, c), load(base1, c), base2[c], load(passed, c)
+        take_y(3, c)
+        u0, u1, v2, q = load(0, c), load(1, c), base2[c], load(3, c)
         values = 2.0 * (inv * q - v2) - (inv * u1 - u0)
         base3[c] = values
         applied = operate(values)
@@ -475,13 +471,14 @@
         add_dot(14, u1, applied)
         add_dot(15, v2, applied)
         add_dot(16, values, applied)
+        pl.when(c == 0)(lambda: pass_on(3, 2))
         return carry
 
     lax.fori_loop(0, 3, turn_3, 0)
     spread_sums(in_row(8, 24), late, 2, me, total, anywhere)
 
     def drain(at, carry):
-        for side, copy in copies(at // 3, at % 3):
+        for side, copy in copies(at // 3, lax.rem(at, 3), SIDES):
             pl.when(exists(side))(copy.wait_send)
         return carry
 
@@ -523,7 +520,7 @@
     put_back = picks.T.astype(bf16)
     put_back = jnp.concatenate([put_back, put_back], axis=1)
     for c in range(3):
-        mixed = weights[0] * load(base0, c) + weights[1] * load(base1, c)
+        mixed = weights[0] * load(0, c) + weights[1] * load(1, c)
         mixed = mixed + weights[2] * base2[c] + weights[3] * base3[c]
         whole = jnp.concatenate([mixed[h] for h in range(4)], axis=1)
         out_ref[c] = dot(put_back, jnp.concatenate(split(whole), axis=0))
@@ -554,22 +551,16 @@
             pltpu.VMEM((4, cells, 128), f32),
             pltpu.VMEM(flat, f32),
             pltpu.VMEM(flat, f32),
-            pltpu.VMEM(brick, f32),
-            pltpu.VMEM(brick, f32),
+            pltpu.VMEM((ITERS,) + brick, f32),
             pltpu.VMEM(flat, f32),
             pltpu.VMEM(flat, f32),
-            pltpu.VMEM(brick, f32),
             pltpu.VMEM((24, 8, 128), f32),
-            pltpu.VMEM((ITERS, 3, 4, EZ, 128), f32),
-            pltpu.VMEM((ITERS, 3, 4, EZ, 128), f32),
             pltpu.VMEM((ITERS, 3, 4, EZ, 128), f32),
             pltpu.VMEM((ITERS, 3, 4, EZ, 128), f32),
             pltpu.VMEM((nx, 1, 128), f32),
             pltpu.VMEM((ny, 1, 128), f32),
             pltpu.VMEM((nx * ny, 1, 128), f32),
             pltpu.SemaphoreType.DMA((6,)),
-            pltpu.SemaphoreType.DMA((ITERS, 3, 4)),
-            pltpu.SemaphoreType.DMA((ITERS, 3, 4)),
             pltpu.SemaphoreType.DMA((ITERS, 3, 4)),
             pltpu.SemaphoreType.DMA((ITERS, 3, 4)),
             pltpu.SemaphoreType.DMA((3,)),

time: 36.7 us -> 47.8 us (1.30)
  Pallas kernels: 34.8 us -> 45.8 us
    pallas_call x1, Pallas kernels: 34.8 us -> 45.8 us  [local(): pl.pallas_call(functools.partial(kernel, nx, ny), out_shape=jax.ShapeDtyp...]
where the time goes in v3:
time: 47.8 us; the launch traced here: 47.6 us
  Pallas kernels  45.8 us (96%)
  local copies, waits for them, and re-layouts  1.77 us (4%)
    pallas_call x1, Pallas kernels, local(): pl.pallas_call(functools.partial(kernel, nx, ny), out_shape=jax.ShapeDtyp...  45.8 us
    unnamed x1, local copies, waits for them, and re-layouts  1.77 us

profile of v3, /device:TPU:0, one launch (start us, length us, event | category | flops | bytes accessed | tf_op | source)
XLA Modules:
  0.0 47.6 jit_solution(17543565083359455511)
XLA Ops:
  0.0 45.8 %shard_map.64 = f32[3,64,512]{2,1,0:T(8,128)} custom-call(f32[3,64,512]{2,1,0:T(8,128)} %bitcast.9, bf16[3,64,512]{2,1,0:T(8,128)(2,1)} %bitcast.11, f32[3,64,512]{2,1,0:T(8,128)} %bitcast.10, f32[1,64,512]{2,1,0:T(8,128)} %bitcast.12, s32[1,64]{1,0:T(1,128)} %bitcast.13, f32[584,128]{1,0:T(8,128)} %constant.2.clone.table_hbm), custom_call_target="tpu_custom_call" | custom-call | tf_op jit(solution)/shard_map/pallas_call | solution.py:537
  45.8 1.8 %copy.9 = f32[3,1,1,64,512]{4,3,2,1,0:T(8,128)} copy(f32[3,1,1,64,512]{4,3,2,1,0:T(8,128)} %bitcast.8) | data formatting | bytes 786432

commit v4 on v2

--- a/solution.py
+++ b/solution.py
@@ -279,8 +279,10 @@
             face_out[turn, c, d] = acc
         for d, side in enumerate(CORNERS):
             h, x, y, start = corner_spot(side)
-            corner_out[turn, c, d] = dest[c, h, x, y]
-        for side, copy in copies(turn, c):
+            line = jnp.where(group == start // 8, dest[c, h, x, y], 0.0)
+            line = pltpu.roll(line, -start % 128, 1, stride=8, stride_axis=0)
+            corner_out[turn, c, d] = jnp.sum(line, axis=0, keepdims=True)
+        for side, copy in reversed(copies(turn, c)):
             pl.when(exists(side))(copy.start)
 
     def take_faces(turn, dest, c):
@@ -299,10 +301,13 @@
                 for x in range(EX):
                     part = roll(arrived, j * 8 - h * 8 - x * 32)
                     dest[c, h, x, y] = dest[c, h, x, y] + jnp.where(lane_j == j, part, 0.0)
+        row_of = lax.broadcasted_iota(jnp.int32, (EZ, 128), 0)
+        own_group = row_of == lax.broadcasted_iota(jnp.int32, (EZ, 128), 1) // 8
         for d, side in enumerate(CORNERS):
             h, x, y, start = corner_spot((-side[0], -side[1]))
-            other = corner_spot(side)[3]
-            part = roll(corner_in[turn, c, d], start - other)
+            part = jnp.where(own_group, corner_in[turn, c, d], 0.0)
+            for shift in (64, 32, 16, 8):
+                part = part + roll(part, shift)
             dest[c, h, x, y] = dest[c, h, x, y] + jnp.where(group == start // 8, part, 0.0)
 
     def operate(values):
@@ -562,8 +567,8 @@
             pltpu.VMEM((24, 8, 128), f32),
             pltpu.VMEM((ITERS, 3, 4, EZ, 128), f32),
             pltpu.VMEM((ITERS, 3, 4, EZ, 128), f32),
-            pltpu.VMEM((ITERS, 3, 4, EZ, 128), f32),
-            pltpu.VMEM((ITERS, 3, 4, EZ, 128), f32),
+            pltpu.VMEM((ITERS, 3, 4, 1, 128), f32),
+            pltpu.VMEM((ITERS, 3, 4, 1, 128), f32),
             pltpu.VMEM((nx, 1, 128), f32),
             pltpu.VMEM((ny, 1, 128), f32),
             pltpu.VMEM((nx * ny, 1, 128), f32),

time: 36.7 us -> 37.6 us (1.025)
  Pallas kernels: 34.8 us -> 35.6 us
    pallas_call x1, Pallas kernels: 34.8 us -> 35.6 us  [local(): pl.pallas_call(functools.partial(kernel, nx, ny), out_shape=jax.ShapeDtyp...]
where the time goes in v4:
time: 37.6 us; the launch traced here: 37.4 us
  Pallas kernels  35.6 us (95%)
  local copies, waits for them, and re-layouts  1.77 us (5%)
    pallas_call x1, Pallas kernels, local(): pl.pallas_call(functools.partial(kernel, nx, ny), out_shape=jax.ShapeDtyp...  35.6 us
    unnamed x1, local copies, waits for them, and re-layouts  1.77 us

profile of v4, /device:TPU:0, one launch (start us, length us, event | category | flops | bytes accessed | tf_op | source)
XLA Modules:
  0.0 37.4 jit_solution(7492391912437832049)
XLA Ops:
  0.0 35.6 %shard_map.64 = f32[3,64,512]{2,1,0:T(8,128)} custom-call(f32[3,64,512]{2,1,0:T(8,128)} %bitcast.9, bf16[3,64,512]{2,1,0:T(8,128)(2,1)} %bitcast.11, f32[3,64,512]{2,1,0:T(8,128)} %bitcast.10, f32[1,64,512]{2,1,0:T(8,128)} %bitcast.12, s32[1,64]{1,0:T(1,128)} %bitcast.13, f32[584,128]{1,0:T(8,128)} %constant.2.clone.table_hbm), custom_call_target="tpu_custom_call" | custom-call | tf_op jit(solution)/shard_map/pallas_call | solution.py:545
  35.6 1.8 %copy.9 = f32[3,1,1,64,512]{4,3,2,1,0:T(8,128)} copy(f32[3,1,1,64,512]{4,3,2,1,0:T(8,128)} %bitcast.8) | data formatting | bytes 786432

commit v5 on v2

--- a/solution.py
+++ b/solution.py
@@ -166,14 +166,25 @@
 
     barrier = pltpu.get_barrier_semaphore()
 
-    def greet(step, carry):
-        other = lax.rem(me + step, total)
-        pl.semaphore_signal(
-            barrier, inc=1, device_id=(other // ny, lax.rem(other, ny)), device_id_type=MESH
-        )
-        return carry
-
-    lax.fori_loop(1, total, greet, 0)
+    def wrap(at, count):
+        return jnp.where(at >= count, at - count, at)
+
+    def everyone_else(act):
+        for step in range(1, ny):
+            act(gx, wrap(gy + step, ny))
+
+        def column(step, carry):
+            other = wrap(gx + step, nx)
+            for across in range(ny):
+                act(other, wrap(gy + across, ny))
+            return carry
+
+        lax.fori_loop(1, nx, column, 0)
+
+    def greet(x, y):
+        pl.semaphore_signal(barrier, inc=1, device_id=(x, y), device_id_type=MESH)
+
+    everyone_else(greet)
     dots[...] = jnp.zeros_like(dots)
 
     lane = lax.broadcasted_iota(jnp.int32, (1, 128), 1)
@@ -333,35 +344,32 @@
         here = lax.broadcasted_iota(jnp.int32, (last - first, 128), 1)
         return jnp.sum(jnp.where(spot == here, sums, 0.0), axis=0, keepdims=True)
 
-    def spread_sums(row, buffer, at, spot, count, device):
+    def spread_sums(row, buffer, at, spot, targets):
         buffer[spot] = row
 
-        def send(step, carry):
+        def send(x, y):
             pltpu.make_async_remote_copy(
                 src_ref=buffer.at[spot],
                 dst_ref=buffer.at[spot],
                 send_sem=sums_s.at[at],
                 recv_sem=sums_r.at[at],
-                device_id=device(step),
+                device_id=(x, y),
                 device_id_type=MESH,
             ).start()
-            return carry
-
-        lax.fori_loop(1, count, send, 0)
+
+        targets(send)
 
     def await_sums(buffer, at, count, sems):
         arrived = buffer.at[pl.ds(0, count - 1)]
         pltpu.make_async_copy(arrived, arrived, sems.at[at]).wait()
 
-    def along_x(step):
-        return lax.rem(gx + step, nx), gy
-
-    def along_y(step):
-        return gx, lax.rem(gy + step, ny)
-
-    def anywhere(step):
-        other = lax.rem(me + step, total)
-        return other // ny, lax.rem(other, ny)
+    def along_x(act):
+        for step in range(1, nx):
+            act(wrap(gx + step, nx), gy)
+
+    def along_y(act):
+        for step in range(1, ny):
+            act(gx, wrap(gy + step, ny))
 
     got_adj.wait()
     adj = [to_brick(adj_ref[c]) for c in range(3)]
@@ -425,13 +433,13 @@
         return carry
 
     lax.fori_loop(0, 3, turn_0, 0)
-    spread_sums(in_row(0, 8), early_x, 0, gx, nx, along_x)
+    spread_sums(in_row(0, 8), early_x, 0, gx, along_x)
 
     def turn_1(c, carry):
         @pl.when(c == 1)
         def _():
             await_sums(early_x, 0, nx, sums_r)
-            spread_sums(jnp.sum(early_x[...], axis=0), early_y, 1, gy, ny, along_y)
+            spread_sums(jnp.sum(early_x[...], axis=0), early_y, 1, gy, along_y)
 
         take_faces(1, base1, c)
         values = load(base1, c)
@@ -478,14 +486,16 @@
         return carry
 
     lax.fori_loop(0, 3, turn_3, 0)
-    spread_sums(in_row(8, 24), late, 2, me, total, anywhere)
-
-    def drain(at, carry):
-        for side, copy in copies(at // 3, at % 3):
-            pl.when(exists(side))(copy.wait_send)
-        return carry
-
-    lax.fori_loop(0, 3 * ITERS, drain, 0)
+    spread_sums(in_row(8, 24), late, 2, me, everyone_else)
+
+    for turn in range(ITERS):
+
+        def drain(c, carry):
+            for side, copy in copies(turn, c):
+                pl.when(exists(side))(copy.wait_send)
+            return carry
+
+        lax.fori_loop(0, 3, drain, 0)
     await_sums(early_x, 0, nx, sums_s)
     await_sums(early_y, 1, ny, sums_s)
 

time: 36.7 us -> 36.7 us (level)
  no operation moved by 1% of the time
where the time goes in v5:
time: 36.7 us; the launch traced here: 36.6 us
  Pallas kernels  34.8 us (95%)
  local copies, waits for them, and re-layouts  1.77 us (5%)
    pallas_call x1, Pallas kernels, local(): pl.pallas_call(functools.partial(kernel, nx, ny), out_shape=jax.ShapeDtyp...  34.8 us
    unnamed x1, local copies, waits for them, and re-layouts  1.77 us

profile of v5, /device:TPU:0, one launch (start us, length us, event | category | flops | bytes accessed | tf_op | source)
XLA Modules:
  0.0 36.6 jit_solution(966263397174656529)
XLA Ops:
  0.0 34.8 %shard_map.64 = f32[3,64,512]{2,1,0:T(8,128)} custom-call(f32[3,64,512]{2,1,0:T(8,128)} %bitcast.9, bf16[3,64,512]{2,1,0:T(8,128)(2,1)} %bitcast.11, f32[3,64,512]{2,1,0:T(8,128)} %bitcast.10, f32[1,64,512]{2,1,0:T(8,128)} %bitcast.12, s32[1,64]{1,0:T(1,128)} %bitcast.13, f32[584,128]{1,0:T(8,128)} %constant.2.clone.table_hbm), custom_call_target="tpu_custom_call" | custom-call | tf_op jit(solution)/shard_map/pallas_call | solution.py:550
  34.8 1.8 %copy.9 = f32[3,1,1,64,512]{4,3,2,1,0:T(8,128)} copy(f32[3,1,1,64,512]{4,3,2,1,0:T(8,128)} %bitcast.8) | data formatting | bytes 786432

commit v6 on v5

--- a/solution.py
+++ b/solution.py
@@ -413,7 +413,8 @@
         send_faces(0, base0, c)
         return carry
 
-    lax.fori_loop(0, 3, first_send, 0)
+    for c in range(3):
+        first_send(c, 0)
 
     got_dif.wait()
     for m in range(3):
@@ -432,7 +433,8 @@
         send_faces(1, base1, c)
         return carry
 
-    lax.fori_loop(0, 3, turn_0, 0)
+    for c in range(3):
+        turn_0(c, 0)
     spread_sums(in_row(0, 8), early_x, 0, gx, along_x)
 
     def turn_1(c, carry):
@@ -450,7 +452,8 @@
         send_faces(2, passed, c)
         return carry
 
-    lax.fori_loop(0, 3, turn_1, 0)
+    for c in range(3):
+        turn_1(c, 0)
     await_sums(early_y, 1, ny, sums_r)
     early = jnp.sum(early_y[...], axis=0)
     norm = early[:, 0:1]
@@ -471,7 +474,8 @@
         send_faces(3, passed, c)
         return carry
 
-    lax.fori_loop(0, 3, turn_2, 0)
+    for c in range(3):
+        turn_2(c, 0)
 
     def turn_3(c, carry):
         take_faces(3, passed, c)
@@ -485,7 +489,8 @@
         add_dot(16, values, applied)
         return carry
 
-    lax.fori_loop(0, 3, turn_3, 0)
+    for c in range(3):
+        turn_3(c, 0)
     spread_sums(in_row(8, 24), late, 2, me, everyone_else)
 
     for turn in range(ITERS):

time: 36.7 us -> 36.6 us (level)
  no operation moved by 1% of the time
where the time goes in v6:
time: 36.6 us; the launch traced here: 36.5 us
  Pallas kernels  34.7 us (95%)
  local copies, waits for them, and re-layouts  1.77 us (5%)
    pallas_call x1, Pallas kernels, local(): pl.pallas_call(functools.partial(kernel, nx, ny), out_shape=jax.ShapeDtyp...  34.7 us
    unnamed x1, local copies, waits for them, and re-layouts  1.77 us

profile of v6, /device:TPU:0, one launch (start us, length us, event | category | flops | bytes accessed | tf_op | source)
XLA Modules:
  0.0 36.5 jit_solution(5528193253449833890)
XLA Ops:
  0.0 34.7 %shard_map.64 = f32[3,64,512]{2,1,0:T(8,128)} custom-call(f32[3,64,512]{2,1,0:T(8,128)} %bitcast.9, bf16[3,64,512]{2,1,0:T(8,128)(2,1)} %bitcast.11, f32[3,64,512]{2,1,0:T(8,128)} %bitcast.10, f32[1,64,512]{2,1,0:T(8,128)} %bitcast.12, s32[1,64]{1,0:T(1,128)} %bitcast.13, f32[584,128]{1,0:T(8,128)} %constant.2.clone.table_hbm), custom_call_target="tpu_custom_call" | custom-call | tf_op jit(solution)/shard_map/pallas_call | solution.py:555
  34.7 1.8 %copy.9 = f32[3,1,1,64,512]{4,3,2,1,0:T(8,128)} copy(f32[3,1,1,64,512]{4,3,2,1,0:T(8,128)} %bitcast.8) | data formatting | bytes 786432
